TPU v7x, 512 devices: a whole 4x8x8 slice. The times are simulated.
512 devices in a mesh: dom: 128 (over z, y, core), hub: 4 (over x).
Axes of the slice: x: 4, y: 8, z: 8, core: 2. Of those that a mesh axis runs over, the one named last changes fastest.
Arguments:
- user_cot: float32 [16384, 256], P('dom'), may hold values from -6 to 6
- hub_adj: float32 [16384, 2048], P('dom', 'hub'), may hold values from -0.09375 to 0.09375
- tiles: float32 [65536, 8, 128], P(('dom', 'hub')), may hold values from -0.125 to 0.125
- tile_index: int32 [3, 65536], P(None, ('dom', 'hub')), may hold values from 0 to 127, as said below
- hub_mask: int32 [2, 2048, 256], P(None, 'hub'), may hold values 0 or 1
- tail_mask: int32 [2, 32768, 256], P(None, 'dom'), may hold values 0 or 1
Outputs:
- user_grad: float32 [16384, 256], P('dom')
- hub_grad: float32 [2048, 256], P('hub')
- tail_grad: float32 [32768, 256], P('dom')
Inputs may be any that keep to these rules, and one draw needn't show every extreme that they name: `tile_index`: row 0 is a tile's user block within its own partition (below 1), row 1 the partition that owns its items (below 128 partitions, i.e. 16384 / 128), row 2 the item block within that partition (below 32). Rows 1 and 2 are the same, position by position, on all 4 hub shards of one partition. No device holds more than 2 tiles whose items one partition owns. One particular partition receives exactly 2 tiles from every device; any other partition receives 0, 1 or 2 tiles from a device.
All inputs are finite; a program needn't handle non-finite values. No bound on the sum of `hub_mask` or of `tail_mask` on one device may be relied on, other than what follows from the above.
Results may differ from a plain program's by a relative error of at most 0.0001.
Values sent between devices are 32-bit elements; how exact they have to be, the bound alone decides.
A program may use at most 64 MiB of HBM per device.

v0:
```python
import jax
import jax.numpy as jnp
from jax import lax
from jax.sharding import PartitionSpec as P

PRECISE = lax.Precision.HIGHEST


def local(user_cot, hub_adj, tiles, tile_index, hub_mask, tail_mask):
    dom_count = lax.axis_size("dom")
    tile_count, item_rows, user_rows = tiles.shape
    user_count, feature_width = user_cot.shape
    user_blocks = user_count // user_rows
    tail_rows = tail_mask.shape[1]
    tail_blocks = tail_rows // item_rows
    capacity = max(2, 2 * tile_count // dom_count)
    slot_count = dom_count * capacity
    user_block = tile_index[0]
    owners = tile_index[1]
    item_block = tile_index[2]
    chosen = (user_block[:, None] == jnp.arange(user_blocks, dtype=jnp.int32)[None, :]).astype(
        jnp.float32
    )
    placed = (chosen[:, None, :, None] * tiles[:, :, None, :]).reshape(
        tile_count * item_rows, user_count
    )
    positions = jnp.arange(tile_count, dtype=jnp.int32)
    before = (owners[:, None] == owners[None, :]) & (positions[None, :] < positions[:, None])
    ranks = jnp.sum(before.astype(jnp.int32), axis=1)
    slot_of = owners * capacity + ranks
    slot_block = jnp.zeros((slot_count,), jnp.int32).at[slot_of].set(item_block)
    block_ids = jnp.arange(tail_blocks, dtype=jnp.int32)
    gradient = user_cot
    hub_item = None
    tail_item = None
    for trip_index in range(hub_mask.shape[0]):
        hub_part = lax.dot_general(
            hub_adj,
            gradient,
            (((0,), (0,)), ((), ())),
            precision=PRECISE,
            preferred_element_type=jnp.float32,
        )
        hub_item = lax.psum(hub_part, "dom") * hub_mask[trip_index].astype(jnp.float32)
        tile_part = jnp.dot(placed, gradient, precision=PRECISE, preferred_element_type=jnp.float32)
        tile_part = tile_part.reshape(tile_count, item_rows * feature_width)
        outgoing = (
            jnp.zeros((slot_count, item_rows * feature_width), jnp.float32)
            .at[slot_of]
            .set(tile_part)
        )
        incoming, got_block = (
            lax.all_to_all(outgoing, "dom", split_axis=0, concat_axis=0, tiled=True),
            lax.all_to_all(slot_block, "dom", split_axis=0, concat_axis=0, tiled=True),
        )
        member = (got_block[None, :] == block_ids[:, None]).astype(jnp.float32)
        tail_part = jnp.dot(member, incoming, precision=PRECISE, preferred_element_type=jnp.float32)
        tail_part = tail_part.reshape(tail_rows, feature_width)
        tail_item = lax.psum(tail_part, "hub") * tail_mask[trip_index].astype(jnp.float32)
        answer = tail_item.reshape(tail_blocks, item_rows * feature_width)[got_block]
        returned = lax.all_to_all(answer, "dom", split_axis=0, concat_axis=0, tiled=True)
        tile_item = returned[slot_of].reshape(tile_count * item_rows, feature_width)
        user_part = jnp.dot(
            hub_adj, hub_item, precision=PRECISE, preferred_element_type=jnp.float32
        )
        user_part = user_part + lax.dot_general(
            placed,
            tile_item,
            (((0,), (0,)), ((), ())),
            precision=PRECISE,
            preferred_element_type=jnp.float32,
        )
        gradient = lax.psum(user_part, "hub")
    return (gradient, hub_item, tail_item)


def solution(mesh):
    return jax.shard_map(
        local,
        mesh=mesh,
        in_specs=(
            P("dom", None),
            P("dom", "hub"),
            P(("dom", "hub"), None, None),
            P(None, ("dom", "hub")),
            P(None, "hub", None),
            P(None, "dom", None),
        ),
        out_specs=(P("dom", None), P("hub", None), P("dom", None)),
        check_vma=False,
    )
```

profile of v0, /device:TPU:1, one launch (start us, length us, event | category | flops | bytes accessed | tf_op | source)
XLA Modules:
  0.0 876.4 jit_solution(14577120800041582356)
XLA Ops:
  8.0 0.8 slice_bitcast_fusion
  8.8 0.2 convert_reduce_fusion
  8.9 0.7 fusion.30
  9.6 1.0 scatter_custom_fusion
  10.6 0.8 all_to_all.41
  11.4 18.4 %all-to-all-start = ((s32[128,2,1]{1,2,0:T(1,128)}), s32[128,2,1]{1,2,0:T(1,128)S(1)}, u32[]{:S(2)}, u32[]{:S(2)}) async-start(s32[128,2,1]{1,2,0:T(1,128)} %bitcast.9), calls=%async_computation | async-start | bytes 131072 | tf_op jit(solution)/shard_map/all_to_all | solution.py:54
  29.8 0.7 fusion.29
  30.5 2.1 fusion.12
  32.6 0.2 reshape.178
  32.8 1.7 scatter_custom_fusion.1
  34.5 2.3 all_to_all.43
  36.8 4.4 all-to-all-done
  41.2 9.3 %all-to-all-start.1 = ((f32[128,2,2048]{2,1,0:T(2,128)}), f32[128,2,2048]{2,1,0:T(2,128)S(1)}, u32[]{:S(2)}, u32[]{:S(2)}) async-start(f32[128,2,2048]{2,1,0:T(2,128)} %all_to_all.43), calls=%async_computation.1 | async-start | bytes 4194304 | tf_op jit(solution)/shard_map/all_to_all | solution.py:53
  50.6 0.5 broadcast.97
  51.1 0.8 reduce.5
  51.9 0.1 eq.56
  52.1 0.1 all_to_all.46
  52.2 49.6 %all-to-all-done.1 = f32[128,2,2048]{2,1,0:T(2,128)S(1)} async-done(((f32[128,2,2048]{2,1,0:T(2,128)}), f32[128,2,2048]{2,1,0:T(2,128)S(1)}, u32[]{:S(2)}, u32[]{:S(2)}) %all-to-all-start.1) | async-done | bytes 2097184 | tf_op jit(solution)/shard_map/all_to_all | solution.py:53
  101.8 2.5 all_to_all.45
  104.3 2.5 fusion.26
  106.8 0.7 reshape.126
  107.6 46.3 %all-reduce.9.cloned.1.call-done = f32[256,256]{1,0:T(8,128)} async-done(((f32[256,256]{1,0:T(8,128)}), f32[256,256]{1,0:T(8,128)}) %all-reduce.9.cloned.1.call-update) | async-done | bytes 262160 | tf_op jit(solution)/shard_map/psum | solution.py:59
  153.9 1.0 bitcast_multiply_fusion.4
  154.9 1.5 gather_fusion
  156.4 2.3 all_to_all.47
  158.7 17.2 %all-to-all-start.2 = ((f32[128,2,2048]{2,1,0:T(2,128)}), f32[128,2,2048]{2,1,0:T(2,128)}, u32[]{:S(2)}, u32[]{:S(2)}) async-start(f32[128,2,2048]{2,1,0:T(2,128)} %all_to_all.47), calls=%async_computation.2 | async-start | bytes 4194304 | tf_op jit(solution)/shard_map/all_to_all | solution.py:61
  175.9 0.0 all-reduce.7.cloned.1.call-start
  175.9 1.4 fusion.33
  177.4 0.0 all-reduce.11.cloned.1.call-start
  177.4 49.5 %all-to-all-done.2 = f32[128,2,2048]{2,1,0:T(2,128)} async-done(((f32[128,2,2048]{2,1,0:T(2,128)}), f32[128,2,2048]{2,1,0:T(2,128)}, u32[]{:S(2)}, u32[]{:S(2)}) %all-to-all-start.2) | async-done | bytes 2097184 | tf_op jit(solution)/shard_map/all_to_all | solution.py:61
  226.9 2.7 all_to_all.49
  229.6 1.9 gather_fusion.1
  231.6 1.5 reshape.128
  233.1 2.0 fusion.10
  235.0 158.1 %all-reduce.7.cloned.1.call-done = f32[512,256]{1,0:T(8,128)} async-done(((f32[512,256]{1,0:T(8,128)}), f32[512,256]{1,0:T(8,128)}) %all-reduce.7.cloned.1.call-update) | async-done | bytes 524304 | tf_op jit(solution)/shard_map/psum | solution.py:44
  393.2 2.7 fusion.1
  395.9 0.0 all-reduce.15.cloned.1.call-start
  396.0 47.8 %all-reduce.11.cloned.1.call-done = f32[128,256]{0,1:T(8,128)} async-done(((f32[128,256]{0,1:T(8,128)}), f32[128,256]{0,1:T(8,128)}) %all-reduce.11.cloned.1.call-update) | async-done | bytes 131088 | tf_op jit(solution)/shard_map/psum | solution.py:73
  443.8 1.9 fusion.8
  445.7 1.1 reshape.186
  446.8 2.4 scatter_custom_fusion.2
  449.2 2.3 all_to_all.50
  451.5 67.7 %all_to_all.61 = f32[128,2,2048]{2,1,0:T(2,128)} all-to-all(f32[128,2,2048]{2,1,0:T(2,128)} %all_to_all.50), channel_id=1, replica_groups=mesh['dom'=128,'hub'=4] {'dom'}, dimensions={0} | all-to-all | bytes 4194304 | tf_op jit(solution)/shard_map/all_to_all | solution.py:53
  519.3 2.7 all_to_all.52
  522.0 0.9 fusion.25
  522.8 0.7 reshape.130
  523.6 45.6 %all-reduce.15.cloned.1.call-done = f32[256,256]{1,0:T(8,128)} async-done(((f32[256,256]{1,0:T(8,128)}), f32[256,256]{1,0:T(8,128)}) %all-reduce.15.cloned.1.call-update) | async-done | bytes 262160 | tf_op jit(solution)/shard_map/psum | solution.py:59
  569.2 1.1 bitcast_multiply_fusion.3
  570.3 1.5 gather_fusion.2
  571.8 2.3 all_to_all.53
  574.0 17.0 %all-to-all-start.4 = ((f32[128,2,2048]{2,1,0:T(2,128)}), f32[128,2,2048]{2,1,0:T(2,128)}, u32[]{:S(2)}, u32[]{:S(2)}) async-start(f32[128,2,2048]{2,1,0:T(2,128)} %all_to_all.53), calls=%async_computation.4 | async-start | bytes 4194304 | tf_op jit(solution)/shard_map/all_to_all | solution.py:61
  591.1 0.0 all-reduce.13.cloned.1.call-start
  591.1 1.4 convolution_bitcast_fusion
  592.6 0.2 copy.33
  592.8 215.7 %all-reduce.13.cloned.1.call-done = f32[512,256]{0,1:T(8,128)} async-done(((f32[512,256]{0,1:T(8,128)}), f32[512,256]{0,1:T(8,128)}) %all-reduce.13.cloned.1.call-update) | async-done | bytes 524304 | tf_op jit(solution)/shard_map/psum | solution.py:44
  808.5 1.9 bitcast_multiply_fusion
  810.5 2.7 all_to_all.55
  813.2 1.9 gather_fusion.3
  815.1 1.4 reshape.132
  816.5 2.0 fusion.6
  818.5 1.2 fusion
  819.8 1.0 copy.30
  820.8 46.8 %all-reduce.17.cloned.1.call-done = f32[128,256]{0,1:T(8,128)} async-done(((f32[128,256]{0,1:T(8,128)}), f32[128,256]{0,1:T(8,128)}) %all-reduce.17.cloned.1.call-update) | async-done | bytes 131088 | tf_op jit(solution)/shard_map/psum | solution.py:73
  867.6 1.7 copy.29
  (32 shorter events, 0.3 us)
Async XLA Ops:
  8.0 167.9 %copy-start = (f32[128,512]{1,0:T(8,128)S(1)}, f32[128,512]{1,0:T(8,128)}, u32[]{:S(2)}) copy-start(f32[128,512]{1,0:T(8,128)} %param.7) | copy-start | bytes 786436
  11.4 29.8 %all-to-all-start = ((s32[128,2,1]{1,2,0:T(1,128)}), s32[128,2,1]{1,2,0:T(1,128)S(1)}, u32[]{:S(2)}, u32[]{:S(2)}) async-start(s32[128,2,1]{1,2,0:T(1,128)} %bitcast.9), calls=%async_computation | async-start | bytes 131072 | tf_op jit(solution)/shard_map/all_to_all | solution.py:54
  41.2 60.6 %all-to-all-start.1 = ((f32[128,2,2048]{2,1,0:T(2,128)}), f32[128,2,2048]{2,1,0:T(2,128)S(1)}, u32[]{:S(2)}, u32[]{:S(2)}) async-start(f32[128,2,2048]{2,1,0:T(2,128)} %all_to_all.43), calls=%async_computation.1 | async-start | bytes 4194304 | tf_op jit(solution)/shard_map/all_to_all | solution.py:53
  50.5 103.4 %all-reduce.9.cloned.1.call-start = ((), (), s32[]{:S(2)}) async-start(), calls=%async_computation.6 | async-start | bytes 524288 | tf_op jit(solution)/shard_map/psum | solution.py:59
  104.3 49.6 %copy-start.5 = (s32[2,256,256]{2,1,0:T(8,128)S(1)}, s32[2,256,256]{2,1,0:T(8,128)}, u32[]{:S(2)}) copy-start(s32[2,256,256]{2,1,0:T(8,128)} %param.11) | copy-start | bytes 1572868
  158.7 17.3 %copy-start.6 = (f32[128,256]{1,0:T(8,128)S(1)}, f32[128,256]{1,0:T(8,128)}, u32[]{:S(2)}) copy-start(f32[128,256]{1,0:T(8,128)} %param.6) | copy-start | bytes 393220
  158.7 68.3 %all-to-all-start.2 = ((f32[128,2,2048]{2,1,0:T(2,128)}), f32[128,2,2048]{2,1,0:T(2,128)}, u32[]{:S(2)}, u32[]{:S(2)}) async-start(f32[128,2,2048]{2,1,0:T(2,128)} %all_to_all.47), calls=%async_computation.2 | async-start | bytes 4194304 | tf_op jit(solution)/shard_map/all_to_all | solution.py:61
  175.9 217.3 %all-reduce.7.cloned.1.call-start = ((), (), s32[]{:S(2)}) async-start(), calls=%async_computation.5 | async-start | bytes 1048576 | tf_op jit(solution)/shard_map/psum | solution.py:44
  177.4 266.4 %all-reduce.11.cloned.1.call-start = ((), (), s32[]{:S(2)}) async-start(), calls=%async_computation.7 | async-start | bytes 262144 | tf_op jit(solution)/shard_map/psum | solution.py:73
  231.6 1.5 copy-start.1
  231.6 161.6 %copy-start.3 = (s32[2,512,256]{2,1,0:T(8,128)S(1)}, s32[2,512,256]{2,1,0:T(8,128)}, u32[]{:S(2)}) copy-start(s32[2,512,256]{2,1,0:T(8,128)} %param.10) | copy-start | bytes 3145732
  395.9 173.3 %all-reduce.15.cloned.1.call-start = ((), (), s32[]{:S(2)}) async-start(), calls=%async_computation.9 | async-start | bytes 524288 | tf_op jit(solution)/shard_map/psum | solution.py:59
  570.2 1.5 copy-start.4
  574.0 17.1 %copy-start.7 = (f32[128,256]{0,1:T(8,128)S(1)}, f32[128,256]{0,1:T(8,128)}, u32[]{:S(2)}) copy-start(f32[128,256]{0,1:T(8,128)} %all-reduce.11.cloned.1.call-done) | copy-start | bytes 393220
  574.0 236.4 %all-to-all-start.4 = ((f32[128,2,2048]{2,1,0:T(2,128)}), f32[128,2,2048]{2,1,0:T(2,128)}, u32[]{:S(2)}, u32[]{:S(2)}) async-start(f32[128,2,2048]{2,1,0:T(2,128)} %all_to_all.53), calls=%async_computation.4 | async-start | bytes 4194304 | tf_op jit(solution)/shard_map/all_to_all | solution.py:61
  591.1 1.5 slice-start
  591.1 217.5 %all-reduce.13.cloned.1.call-start = ((), (), s32[]{:S(2)}) async-start(), calls=%async_computation.8 | async-start | bytes 1048576 | tf_op jit(solution)/shard_map/psum | solution.py:44
  592.5 275.1 %all-reduce.17.cloned.1.call-start = ((), (), s32[]{:S(2)}) async-start(), calls=%async_computation.10 | async-start | bytes 262144 | tf_op jit(solution)/shard_map/psum | solution.py:73
  815.1 3.4 copy-start.2
Sparse Core Ops, SparseCore 0:
  107.7 46.1 all-reduce.8
  396.0 47.6 all-reduce.10
  523.7 45.3 all-reduce.14
  819.9 47.6 all-reduce.16
Sparse Core Ops, SparseCore 1:
  180.5 212.6 all-reduce.6
  595.7 212.8 all-reduce.12
where the time goes:
time: 879 us; the launch traced here: 876 us
  waiting for transfers between devices  664 us (76%)
  blocking collectives  67.7 us (8%)
  starting transfers between devices  62.2 us (7%)
  local copies, waits for them, and re-layouts  42.6 us (5%)
  matrix products  18 us (2%)
  between operations  15.5 us (2%)
    psum x2, waiting for transfers between devices, local(): lax.psum(hub_part, 'dom') * hub_mask[trip_index].astype(jnp.float32)  374 us
    psum x2, waiting for transfers between devices, local(): gradient = lax.psum(user_part, 'hub')  94.6 us
    psum x2, waiting for transfers between devices, local(): lax.psum(tail_part, 'hub') * tail_mask[trip_index].astype(jnp.float32)  91.9 us
    all_to_all x1, blocking collectives, local(): lax.all_to_all(outgoing, 'dom', split_axis=0, concat_axis=0, tiled=True)  67.7 us
    all_to_all x1, waiting for transfers between devices, local(): lax.all_to_all(outgoing, 'dom', split_axis=0, concat_axis=0, tiled=True)  49.6 us
    all_to_all x2, waiting for transfers between devices, local(): lax.all_to_all(answer, 'dom', split_axis=0, concat_axis=0, tiled=True)  49.5 us
    all_to_all x2, starting transfers between devices, local(): lax.all_to_all(answer, 'dom', split_axis=0, concat_axis=0, tiled=True)  34.2 us
    all_to_all x1, starting transfers between devices, local(): lax.all_to_all(slot_block, 'dom', split_axis=0, concat_axis=0, tiled=True)  18.4 us
  transfers between devices with their start and end apart: 10, of which 9 were waited for; matrix products, arithmetic and copies ran while one was open for 2% of the time, Pallas kernels for 0%

commit v1 on v0

v1 whole, which is shorter than its diff:
```python
import jax
import jax.numpy as jnp
from jax import lax
from jax.experimental import pallas as pl
from jax.experimental.pallas import tpu as pltpu
from jax.sharding import PartitionSpec as P

F32 = jnp.float32
BF16 = jnp.bfloat16
MESH = pl.DeviceIdType.MESH

(PAIR_RS, ONE_RS, TWO_RS, TWO_AG, ONE_AG, PAIR_AG, TAIL_F, TAIL_R, HUB_RS, HUB_AG, TAIL_OUT, TILE_RS, TILE_AG, INDEX) = range(14)
KINDS = 14


def split(x):
    hi = x.astype(BF16)
    return hi, (x - hi.astype(F32)).astype(BF16)


def dot(a, b, dims=((1,), (0,))):
    return lax.dot_general(a, b, (dims, ((), ())), preferred_element_type=F32)


def dot3(ah, al, bh, bl):
    return dot(ah, bh) + dot(ah, bl) + dot(al, bh)


def lanes(shape):
    return lax.broadcasted_iota(jnp.int32, shape, len(shape) - 1)


def rows(shape):
    return lax.broadcasted_iota(jnp.int32, shape, len(shape) - 2)


def roll64(x):
    return pltpu.roll(x, 64, 1)


def side_by_side(hi, lo):
    return jnp.concatenate([hi, lo], axis=1)


def fold(x):
    return x[:, :128] + x[:, 128:]


def kernel(
    cot_ref, hub_adj_ref, tiles_ref, index_ref, hub_mask_ref, tail_mask_ref,
    user_out, hub_out, tail_out,
    tile_in, tile_sum, slot_index, index_in, tile_hi, tile_lo, tile_t_hi, tile_t_lo, member, member_t,
    hubp, pair_in, one_out, one_in, two_out, two_in, hub_full,
    tail_send, tail_recv, reply_send, reply_recv, user_pack, user_in, grad_pack, tail_pack, grad_ref,
    send_sem, recv_sem,
):
    d = lax.axis_index("dom")
    j = lax.axis_index("hub")
    core = lax.rem(d, 2)
    y = lax.rem(d // 2, 8)
    z = d // 16
    a1 = y * (1 - core) + z * core
    a2 = z * (1 - core) + y * core
    stride1 = 2 * (1 - core) + 16 * core
    stride2 = 16 * (1 - core) + 2 * core
    base1 = d - a1 * stride1
    base2 = d - a2 * stride2
    partner = d + 1 - 2 * core

    def send(src, dst, t, kind, dom, hub):
        pltpu.make_async_remote_copy(
            src_ref=src, dst_ref=dst, send_sem=send_sem.at[t, kind], recv_sem=recv_sem.at[t, kind],
            device_id=(dom, hub), device_id_type=MESH,
        ).start()

    def wait_in(ref, t, kind):
        pltpu.make_async_copy(ref, ref, recv_sem.at[t, kind]).wait()

    def wait_out(ref, t, kind):
        pltpu.make_async_copy(ref, ref, send_sem.at[t, kind]).wait()

    def peers_all(body):
        def step(k, carry):
            body(lax.rem(d + k, 128))
            body(lax.rem(d + 128 - k, 128))
            return carry
        lax.fori_loop(1, 64, step, 0)
        body(lax.rem(d + 64, 128))

    def peers_hub(body):
        for o in (1, 3, 2):
            body(lax.rem(j + o, 4), o - 1)

    barrier = pltpu.get_barrier_semaphore()
    peers_all(lambda p: pl.semaphore_signal(barrier, inc=1, device_id=(p, j), device_id_type=MESH))
    peers_hub(lambda h, o: pl.semaphore_signal(barrier, inc=1, device_id=(d, h), device_id_type=MESH))
    pl.semaphore_wait(barrier, 130)

    peers_hub(lambda h, o: send(tiles_ref.at[pl.ds(h * 32, 32)], tile_in.at[o], 0, TILE_RS, d, h))

    owner_row = jnp.broadcast_to(index_ref[1:2, :], (128, 128))
    block_row = jnp.broadcast_to(index_ref[2:3, :], (128, 128)).astype(F32)
    square = (128, 128)
    earlier = (owner_row == owner_row.astype(F32).T.astype(jnp.int32)) & (rows(square) < lanes(square))
    rank = jnp.sum(earlier.astype(F32), axis=0, keepdims=True)
    owned = owner_row == rows(square)
    pick0 = (owned & (rank < 0.5)).astype(F32)
    pick1 = (owned & (rank > 0.5)).astype(F32)
    block0 = jnp.sum(pick0 * block_row, axis=1, keepdims=True)
    block1 = jnp.sum(pick1 * block_row, axis=1, keepdims=True)
    slot_index[...] = jnp.where(lanes(square) < 64, block0, block1).reshape(128, 1, 128)
    index_in[pl.ds(d, 1)] = slot_index[pl.ds(d, 1)]
    peers_all(lambda p: send(slot_index.at[p], index_in.at[d], 0, INDEX, p, j))

    adj = hub_adj_ref[...]
    adj_hi, adj_lo = split(adj)
    adj_t_hi, adj_t_lo = split(adj.T)

    def hub_start(t, grad):
        gh, gl = split(grad)
        hubp[t] = dot3(adj_t_hi, adj_t_lo, gh, gl)
        send(hubp.at[t, pl.ds((1 - core) * 256, 256)], pair_in.at[t], t, PAIR_RS, partner, j)

    def hub_one(t):
        wait_in(pair_in.at[t], t, PAIR_RS)
        one_out[t] = (hubp[t, pl.ds(core * 256, 256)] + pair_in[t]).reshape(8, 32, 256)
        for o in (1, 7, 2, 6, 3, 5, 4):
            g = lax.rem(a1 + o, 8)
            send(one_out.at[t, g], one_in.at[t, o - 1], t, ONE_RS, base1 + g * stride1, j)

    def hub_two(t):
        wait_in(one_in.at[t], t, ONE_RS)
        total = one_out[t, a1]
        for o in range(7):
            total = total + one_in[t, o]
        for b in range(4):
            for h in range(2):
                two_out[t, 2 * b + h] = total[8 * b:8 * b + 8, 128 * h:128 * h + 128]
        for o in (1, 7, 2, 6, 3, 5, 4):
            g = lax.rem(a2 + o, 8)
            send(two_out.at[t, g], two_in.at[t, o - 1], t, TWO_RS, base2 + g * stride2, j)

    def hub_back_two(t):
        wait_in(two_in.at[t], t, TWO_RS)
        total = two_out[t, a2]
        for o in range(7):
            total = total + two_in[t, o]
        first = pl.multiple_of(core * 256 + a1 * 32 + (a2 // 2) * 8, 8)
        left = pl.multiple_of(lax.rem(a2, 2) * 128, 128)
        mask = hub_mask_ref[t, pl.ds(first, 8), pl.ds(left, 128)].astype(F32)
        hub_full[t, core, a1, a2] = total * mask
        for o in (1, 7, 2, 6, 3, 5, 4):
            g = lax.rem(a2 + o, 8)
            send(hub_full.at[t, core, a1, a2], hub_full.at[t, core, a1, a2], t, TWO_AG, base2 + g * stride2, j)

    def hub_back_one(t):
        wait_in(two_in.at[t], t, TWO_AG)
        for o in (1, 7, 2, 6, 3, 5, 4):
            g = lax.rem(a1 + o, 8)
            send(hub_full.at[t, core, a1], hub_full.at[t, core, a1], t, ONE_AG, base1 + g * stride1, j)

    def hub_back_pair(t):
        wait_in(one_in.at[t], t, ONE_AG)
        send(hub_full.at[t, core], hub_full.at[t, core], t, PAIR_AG, partner, j)

    def hub_finish(t):
        wait_in(pair_in.at[t], t, PAIR_AG)
        full = hub_full[t].reshape(64, 2, 8, 128)
        item = jnp.concatenate([full[:, 0].reshape(512, 128), full[:, 1].reshape(512, 128)], axis=1)
        if t == 1:
            hub_out[...] = item
        ih, il = split(item)
        part = dot3(adj_hi, adj_lo, ih, il)
        low = lanes((64, 128)) < 64
        for h in range(4):
            half = part[:, 128 * (h // 2):128 * (h // 2) + 128]
            if h % 2 == 0:
                user_pack[t, h] = jnp.where(low, half[:64], roll64(half[64:]))
            else:
                user_pack[t, h] = jnp.where(low, roll64(half[:64]), half[64:])
        peers_hub(lambda h, o: send(user_pack.at[t, h], user_in.at[t, o], t, HUB_RS, d, h))

    left_half = pl.multiple_of((j // 2) * 128, 128)
    odd = lax.rem(j, 2)

    def mine(half):
        kept = jnp.where((lanes(half.shape) // 64) == odd, half, 0.0)
        return kept + roll64(kept)

    def halves(x):
        low = lanes(x.shape) < 64
        return jnp.concatenate([jnp.where(low, x, 0.0), jnp.where(low, 0.0, x)], axis=0)

    def tail_start(t, half):
        bh, bl = split(halves(mine(half)))
        both = side_by_side(bh, bl)
        for q in range(4):
            part = slice(256 * q, 256 * q + 256)
            x = fold(dot(tile_hi[part], both)) + dot(tile_lo[part], bh)
            tail_send[t, 32 * q:32 * q + 32] = x.reshape(32, 8, 128)
        tail_recv[t, d] = tail_send[t, d]
        peers_all(lambda p: send(tail_send.at[t, p], tail_recv.at[t, d], t, TAIL_F, p, j))

    def tail_turn(t):
        wait_in(tail_recv.at[t, pl.ds(0, 127)], t, TAIL_F)
        hi, lo = split(tail_recv[t].reshape(1024, 128))
        x = fold(dot(member[...], side_by_side(hi, lo)))
        low = lanes((256, 128)) < 64
        item = jnp.where(low, x[:256], x[256:])
        item = item + roll64(item)
        item = item * mine(tail_mask_ref[t, :, pl.ds(left_half, 128)].astype(F32))
        ih, il = split(halves(item))
        both = side_by_side(ih, il)
        for q in range(4):
            x = fold(dot(member_t[256 * q:256 * q + 256], both))
            reply_send[t, 32 * q:32 * q + 32] = x.reshape(32, 8, 128)
        reply_recv[t, d] = reply_send[t, d]
        peers_all(lambda p: send(reply_send.at[t, p], reply_recv.at[t, d], t, TAIL_R, p, j))
        if t == 1:
            tail_pack[j] = jnp.where(lanes((128, 128)) < 64, item[:128], item[128:])
            peers_hub(lambda h, o: send(tail_pack.at[j], tail_pack.at[j], 0, TAIL_OUT, d, h))

    def tail_end(t):
        wait_in(reply_recv.at[t, pl.ds(0, 127)], t, TAIL_R)
        rh, rl = split(reply_recv[t].reshape(1024, 128))
        x = fold(dot(tile_t_hi[...], side_by_side(rh, rl))) + dot(tile_t_lo[...], rh)
        low = lanes((64, 128)) < 64
        return jnp.where(low, x[:64] + roll64(x[128:192]), roll64(x[64:128]) + x[192:])

    def join(t, packed):
        wait_in(user_in.at[t], t, HUB_RS)
        grad_pack[t, j] = packed + user_pack[t, j] + user_in[t, 0] + user_in[t, 1] + user_in[t, 2]
        peers_hub(lambda h, o: send(grad_pack.at[t, j], grad_pack.at[t, j], t, HUB_AG, d, h))
        wait_in(user_in.at[t], t, HUB_AG)
        low = lanes((64, 128)) < 64
        out = user_out if t == 1 else grad_ref
        for k in range(2):
            even, uneven = grad_pack[t, 2 * k], grad_pack[t, 2 * k + 1]
            out[:64, 128 * k:128 * k + 128] = jnp.where(low, even, roll64(uneven))
            out[64:, 128 * k:128 * k + 128] = jnp.where(low, roll64(even), uneven)

    hub_start(0, cot_ref[...])
    wait_in(tile_in, 0, TILE_RS)
    own = pl.ds(j * 32, 32)
    tile_sum[own] = tiles_ref[own] + tile_in[0] + tile_in[1] + tile_in[2]
    peers_hub(lambda h, o: send(tile_sum.at[own], tile_sum.at[own], 0, TILE_AG, d, h))
    hub_one(0)
    wait_in(tile_in, 0, TILE_AG)

    th, tl = split(tile_sum[...].reshape(128, 1024))
    both = jnp.concatenate([th, tl], axis=1)
    for s, pick in ((0, pick0), (1, pick1)):
        x = dot(pick.astype(BF16), both)
        placed = (x[:, :1024] + x[:, 1024:]).reshape(1024, 128)
        hi, lo = split(placed)
        tile_hi[:, 128 * s:128 * s + 128] = hi
        tile_lo[:, 128 * s:128 * s + 128] = lo
        hi, lo = split(placed.T)
        tile_t_hi[128 * s:128 * s + 128] = hi
        tile_t_lo[128 * s:128 * s + 128] = lo
    tail_start(0, cot_ref[:, pl.ds(left_half, 128)])
    hub_two(0)

    wait_in(index_in.at[pl.ds(0, 127)], 0, INDEX)
    spread = (rows((1024, 128)) // 8 == lanes((1024, 128))).astype(BF16)
    blocks = dot(spread, index_in[...].reshape(128, 128).astype(BF16))
    place = blocks * 8.0 + lax.rem(rows((1024, 128)), 8).astype(F32)
    place_t = place.T
    want_t = lanes((1024, 256)).astype(F32)
    want = rows((256, 1024)).astype(F32)
    for s in range(2):
        member_t[:, 256 * s:256 * s + 256] = (place[:, 64 * s:64 * s + 1] == want_t).astype(F32).astype(BF16)
        member[256 * s:256 * s + 256] = (place_t[64 * s:64 * s + 1] == want).astype(F32).astype(BF16)

    for t in range(2):
        if t == 1:
            hub_start(1, grad_ref[...])
            tail_start(1, grad_ref[:, pl.ds(left_half, 128)])
            hub_one(1)
            hub_two(1)
        hub_back_two(t)
        hub_back_one(t)
        hub_back_pair(t)
        tail_turn(t)
        hub_finish(t)
        join(t, tail_end(t))

    wait_in(tail_pack.at[pl.ds(0, 3)], 0, TAIL_OUT)
    low = lanes((128, 128)) < 64
    for k in range(2):
        even, uneven = tail_pack[2 * k], tail_pack[2 * k + 1]
        tail_out[:128, 128 * k:128 * k + 128] = jnp.where(low, even, roll64(uneven))
        tail_out[128:, 128 * k:128 * k + 128] = jnp.where(low, roll64(even), uneven)

    wait_out(tile_in, 0, TILE_RS)
    wait_out(tile_in, 0, TILE_AG)
    wait_out(index_in.at[pl.ds(0, 127)], 0, INDEX)
    wait_out(tail_pack.at[pl.ds(0, 3)], 0, TAIL_OUT)
    for t in range(2):
        wait_out(pair_in.at[t], t, PAIR_RS)
        wait_out(one_in.at[t], t, ONE_RS)
        wait_out(two_in.at[t], t, TWO_RS)
        wait_out(two_in.at[t], t, TWO_AG)
        wait_out(one_in.at[t], t, ONE_AG)
        wait_out(pair_in.at[t], t, PAIR_AG)
        wait_out(tail_recv.at[t, pl.ds(0, 127)], t, TAIL_F)
        wait_out(reply_recv.at[t, pl.ds(0, 127)], t, TAIL_R)
        wait_out(user_in.at[t], t, HUB_RS)
        wait_out(user_in.at[t], t, HUB_AG)


def local(user_cot, hub_adj, tiles, tile_index, hub_mask, tail_mask):
    vmem = pl.BlockSpec(memory_space=pltpu.VMEM)
    return pl.pallas_call(
        kernel,
        out_shape=(
            jax.ShapeDtypeStruct((128, 256), F32),
            jax.ShapeDtypeStruct((512, 256), F32),
            jax.ShapeDtypeStruct((256, 256), F32),
        ),
        in_specs=[vmem] * 6,
        out_specs=(vmem,) * 3,
        scratch_shapes=[
            pltpu.VMEM((3, 32, 8, 128), F32),
            pltpu.VMEM((128, 8, 128), F32),
            pltpu.VMEM((128, 1, 128), F32),
            pltpu.VMEM((128, 1, 128), F32),
            pltpu.VMEM((1024, 256), BF16),
            pltpu.VMEM((1024, 256), BF16),
            pltpu.VMEM((256, 1024), BF16),
            pltpu.VMEM((256, 1024), BF16),
            pltpu.VMEM((512, 1024), BF16),
            pltpu.VMEM((1024, 512), BF16),
            pltpu.VMEM((2, 512, 256), F32),
            pltpu.VMEM((2, 256, 256), F32),
            pltpu.VMEM((2, 8, 32, 256), F32),
            pltpu.VMEM((2, 7, 32, 256), F32),
            pltpu.VMEM((2, 8, 8, 128), F32),
            pltpu.VMEM((2, 7, 8, 128), F32),
            pltpu.VMEM((2, 2, 8, 8, 8, 128), F32),
            pltpu.VMEM((2, 128, 8, 128), F32),
            pltpu.VMEM((2, 128, 8, 128), F32),
            pltpu.VMEM((2, 128, 8, 128), F32),
            pltpu.VMEM((2, 128, 8, 128), F32),
            pltpu.VMEM((2, 4, 64, 128), F32),
            pltpu.VMEM((2, 3, 64, 128), F32),
            pltpu.VMEM((2, 4, 64, 128), F32),
            pltpu.VMEM((4, 128, 128), F32),
            pltpu.VMEM((128, 256), F32),
            pltpu.SemaphoreType.DMA((2, KINDS)),
            pltpu.SemaphoreType.DMA((2, KINDS)),
        ],
        compiler_params=pltpu.CompilerParams(
            collective_id=0, has_side_effects=True, vmem_limit_bytes=48 * 1024 * 1024
        ),
        cost_estimate=pl.CostEstimate(flops=4_000_000_000, bytes_accessed=4_000_000, transcendentals=0),
    )(user_cot, hub_adj, tiles, tile_index, hub_mask, tail_mask)


def solution(mesh):
    return jax.shard_map(
        local,
        mesh=mesh,
        in_specs=(
            P("dom", None),
            P("dom", "hub"),
            P(("dom", "hub"), None, None),
            P(None, ("dom", "hub")),
            P(None, "hub", None),
            P(None, "dom", None),
        ),
        out_specs=(P("dom", None), P("hub", None), P("dom", None)),
        check_vma=False,
    )
```

time: 879 us -> 147 us (0.17)
  waiting for transfers between devices: 664 us -> 0 us
  Pallas kernels: 0 us -> 138 us
  blocking collectives: 67.7 us -> 0 us
  starting transfers between devices: 62.2 us -> 0 us
  local copies, waits for them, and re-layouts: 42.6 us -> 7.99 us
  matrix products: 18 us -> 0 us
  between operations: 15.5 us -> 0.65 us
    psum x6 -> x0, waiting for transfers between devices: 560 us -> none  [the longest x2 374 us: local(): lax.psum(hub_part, 'dom') * hub_mask[trip_index].astype(jnp.float32)]
    pallas_call x0 -> x1, Pallas kernels: none -> 138 us  [local(): pl.pallas_call(kernel, out_shape=(jax.ShapeDtypeStruct((128, 256), F32),...]
    all_to_all x4 -> x0, waiting for transfers between devices: 104 us -> none  [the longest x1 49.6 us: local(): lax.all_to_all(outgoing, 'dom', split_axis=0, concat_axis=0, tiled=True)]
    all_to_all x1 -> x0, blocking collectives: 67.7 us -> none  [local(): lax.all_to_all(outgoing, 'dom', split_axis=0, concat_axis=0, tiled=True)]
    all_to_all x4 -> x0, starting transfers between devices: 61.9 us -> none  [the longest x2 34.2 us: local(): lax.all_to_all(answer, 'dom', split_axis=0, concat_axis=0, tiled=True)]
    all_to_all x11 -> x0, local copies, waits for them, and re-layouts: 21.1 us -> none  [the longest x4 9.9 us: local(): lax.all_to_all(answer, 'dom', split_axis=0, concat_axis=0, tiled=True)]
    dot_general x10 -> x0, matrix products: 18 us -> none  [the longest x2 4 us: local(): jnp.dot(placed, gradient, precision=PRECISE, preferred_element_type=jnp.f...]
  transfers between devices with their start and end apart: 10 -> 0, of which waited for: 9 -> 0; matrix products, arithmetic and copies ran while one was open for 2% -> 0% of each run, Pallas kernels for 0% -> 0%
where the time goes in v1:
time: 147 us; the launch traced here: 146 us
  Pallas kernels  138 us (94%)
  local copies, waits for them, and re-layouts  7.99 us (5%)
    pallas_call x1, Pallas kernels, local(): pl.pallas_call(kernel, out_shape=(jax.ShapeDtypeStruct((128, 256), F32),...  138 us
    unnamed x15, local copies, waits for them, and re-layouts  7.99 us

profile of v1, /device:TPU:1, one launch (start us, length us, event | category | flops | bytes accessed | tf_op | source)
XLA Modules:
  0.0 146.5 jit_solution(14460769848699758264)
XLA Ops:
  0.6 0.0 copy-start
  0.6 1.2 copy-done
  1.9 0.0 copy-start.1
  1.9 1.0 copy-done.1
  2.9 0.0 copy-start.2
  2.9 1.0 copy-done.2
  3.9 0.0 copy-start.3
  3.9 0.9 copy-done.3
  4.9 0.0 copy-start.4
  4.9 0.9 copy-done.4
  5.8 0.0 copy-start.5
  5.8 0.7 copy-done.5
  6.5 137.8 %shard_map.85 = (f32[128,256]{1,0:T(8,128)S(1)}, f32[512,256]{1,0:T(8,128)S(1)}, f32[256,256]{1,0:T(8,128)S(1)}) custom-call(f32[128,256]{1,0:T(8,128)S(1)} %copy-done.4, f32[128,512]{1,0:T(8,128)S(1)} %copy-done.3, f32[128,8,128]{2,1,0:T(8,128)S(1)} %copy-done.1, s32[3,128]{1,0:T(4,128)S(1)} %copy-done.5, s32[2,512,256]{2,1,0:T(8,128)S(1)} %copy-done, ...), custom_call_target="tpu_custom_call" | custom-call | flops 4000000000 | bytes 4000000 | tf_op jit(solution)/shard_map/pallas_call | solution.py:314
  144.3 0.7 copy.12
  145.0 0.8 copy.13
  145.8 0.7 copy.14
Async XLA Ops:
  0.6 1.2 copy-start
  1.9 1.0 copy-start.1
  2.9 1.0 copy-start.2
  3.9 0.9 copy-start.3
  4.9 0.9 copy-start.4
  5.8 0.7 copy-start.5

commit v2 on v1

--- a/solution.py
+++ b/solution.py
@@ -9,8 +9,11 @@
 BF16 = jnp.bfloat16
 MESH = pl.DeviceIdType.MESH
 
-(PAIR_RS, ONE_RS, TWO_RS, TWO_AG, ONE_AG, PAIR_AG, TAIL_F, TAIL_R, HUB_RS, HUB_AG, TAIL_OUT, TILE_RS, TILE_AG, INDEX) = range(14)
-KINDS = 14
+(PAIR_RS, ONE_RS, TWO_RS, TWO_AG, ONE_AG, PAIR_AG, TAIL_F, TAIL_R,
+ HUB_RS, HUB_AG, TAIL_OUT, INDEX_ONE, INDEX_TWO, TILE_RS, TILE_AG) = range(15)
+CUTS = 4
+KINDS = 14 + 2 * CUTS
+AROUND = (4, 1, 7, 3, 5, 2, 6)
 
 
 def split(x):
@@ -47,9 +50,10 @@
 
 
 def kernel(
-    cot_ref, hub_adj_ref, tiles_ref, index_ref, hub_mask_ref, tail_mask_ref,
+    cot_hbm, hub_adj_hbm, tiles_hbm, index_hbm, hub_mask_hbm, tail_mask_hbm,
     user_out, hub_out, tail_out,
-    tile_in, tile_sum, slot_index, index_in, tile_hi, tile_lo, tile_t_hi, tile_t_lo, member, member_t,
+    cot_ref, hub_adj_ref, tiles_ref, index_ref, hub_mask_ref, tail_mask_ref, load_sem,
+    tile_in, tile_sum, slot_index, index_mid, index_in, tile_hi, tile_lo, tile_t_hi, tile_t_lo, member, member_t,
     hubp, pair_in, one_out, one_in, two_out, two_in, hub_full,
     tail_send, tail_recv, reply_send, reply_recv, user_pack, user_in, grad_pack, tail_pack, grad_ref,
     send_sem, recv_sem,
@@ -79,24 +83,54 @@
     def wait_out(ref, t, kind):
         pltpu.make_async_copy(ref, ref, send_sem.at[t, kind]).wait()
 
-    def peers_all(body):
+    def around(body, parts=(0, 1)):
+        def both(dz, dy):
+            chip = 16 * lax.rem(z + dz + 8, 8) + 2 * lax.rem(y + dy + 8, 8)
+            body(chip + core)
+            body(chip + 1 - core)
+
         def step(k, carry):
-            body(lax.rem(d + k, 128))
-            body(lax.rem(d + 128 - k, 128))
+            kk = 14 - k + (14 - k) // 12
+            a, b = kk // 4 + 1, lax.rem(kk, 4)
+            both(a, b)
+            both(-b, a)
+            both(-a, -b)
+            both(b, -a)
             return carry
-        lax.fori_loop(1, 64, step, 0)
-        body(lax.rem(d + 64, 128))
+
+        if 0 in parts:
+            both(4, 4)
+            both(4, 0)
+            both(0, 4)
+            lax.fori_loop(0, 7, step, 0)
+        if 1 in parts:
+            lax.fori_loop(7, 15, step, 0)
+            body(partner)
 
     def peers_hub(body):
         for o in (1, 3, 2):
             body(lax.rem(j + o, 4), o - 1)
 
+    loads = [
+        pltpu.make_async_copy(src, dst, load_sem.at[i])
+        for i, (src, dst) in enumerate((
+            (tiles_hbm, tiles_ref), (index_hbm, index_ref), (cot_hbm, cot_ref),
+            (hub_adj_hbm, hub_adj_ref), (hub_mask_hbm, hub_mask_ref), (tail_mask_hbm, tail_mask_ref),
+        ))
+    ]
+    for load in loads:
+        load.start()
     barrier = pltpu.get_barrier_semaphore()
-    peers_all(lambda p: pl.semaphore_signal(barrier, inc=1, device_id=(p, j), device_id_type=MESH))
+    around(lambda p: pl.semaphore_signal(barrier, inc=1, device_id=(p, j), device_id_type=MESH))
     peers_hub(lambda h, o: pl.semaphore_signal(barrier, inc=1, device_id=(d, h), device_id_type=MESH))
+    for load in loads:
+        load.wait()
     pl.semaphore_wait(barrier, 130)
 
-    peers_hub(lambda h, o: send(tiles_ref.at[pl.ds(h * 32, 32)], tile_in.at[o], 0, TILE_RS, d, h))
+    cut = 32 // CUTS
+    for i in range(CUTS):
+        peers_hub(lambda h, o: send(
+            tiles_ref.at[pl.ds(h * 32 + i * cut, cut)], tile_in.at[i, o], 0, TILE_RS + 2 * i, d, h))
 
     owner_row = jnp.broadcast_to(index_ref[1:2, :], (128, 128))
     block_row = jnp.broadcast_to(index_ref[2:3, :], (128, 128)).astype(F32)
@@ -108,9 +142,30 @@
     pick1 = (owned & (rank > 0.5)).astype(F32)
     block0 = jnp.sum(pick0 * block_row, axis=1, keepdims=True)
     block1 = jnp.sum(pick1 * block_row, axis=1, keepdims=True)
-    slot_index[...] = jnp.where(lanes(square) < 64, block0, block1).reshape(128, 1, 128)
-    index_in[pl.ds(d, 1)] = slot_index[pl.ds(d, 1)]
-    peers_all(lambda p: send(slot_index.at[p], index_in.at[d], 0, INDEX, p, j))
+    def ways(p):
+        c, py, pz = lax.rem(p, 2), lax.rem(p // 2, 8), p // 16
+        return c, py * (1 - c) + pz * c, pz * (1 - c) + py * c
+
+    second = 2 * ways(rows(square))[2]
+    spot = jnp.where(lanes(square) == second, block0, 0.0) + jnp.where(lanes(square) == second + 1, block1, 0.0)
+    at_core, at_one, _ = ways(lanes((16, 128)))
+    gather = (8 * at_core + at_one == rows((16, 128))).astype(BF16)
+    slot_index[...] = dot(gather, spot.astype(BF16)).reshape(2, 8, 1, 128)
+
+    def go_one(sources, mid, t, kind):
+        for o in AROUND:
+            g, h = lax.rem(y + o, 8), lax.rem(z + o, 8)
+            send(sources.at[0, g], mid.at[2 * y + core], t, kind, 16 * z + 2 * g, j)
+            send(sources.at[1, h], mid.at[2 * z + core], t, kind, 16 * h + 2 * y + 1, j)
+        send(sources.at[1 - core, a2], mid.at[2 * a2 + core], t, kind, partner, j)
+        mid[2 * a1 + core] = sources[core, a1]
+
+    def along_two(body):
+        for o in AROUND:
+            g = lax.rem(a2 + o, 8)
+            body(g, base2 + g * stride2)
+
+    go_one(slot_index, index_mid, 0, INDEX_ONE)
 
     adj = hub_adj_ref[...]
     adj_hi, adj_lo = split(adj)
@@ -124,7 +179,7 @@
     def hub_one(t):
         wait_in(pair_in.at[t], t, PAIR_RS)
         one_out[t] = (hubp[t, pl.ds(core * 256, 256)] + pair_in[t]).reshape(8, 32, 256)
-        for o in (1, 7, 2, 6, 3, 5, 4):
+        for o in AROUND:
             g = lax.rem(a1 + o, 8)
             send(one_out.at[t, g], one_in.at[t, o - 1], t, ONE_RS, base1 + g * stride1, j)
 
@@ -136,7 +191,7 @@
         for b in range(4):
             for h in range(2):
                 two_out[t, 2 * b + h] = total[8 * b:8 * b + 8, 128 * h:128 * h + 128]
-        for o in (1, 7, 2, 6, 3, 5, 4):
+        for o in AROUND:
             g = lax.rem(a2 + o, 8)
             send(two_out.at[t, g], two_in.at[t, o - 1], t, TWO_RS, base2 + g * stride2, j)
 
@@ -149,13 +204,13 @@
         left = pl.multiple_of(lax.rem(a2, 2) * 128, 128)
         mask = hub_mask_ref[t, pl.ds(first, 8), pl.ds(left, 128)].astype(F32)
         hub_full[t, core, a1, a2] = total * mask
-        for o in (1, 7, 2, 6, 3, 5, 4):
+        for o in AROUND:
             g = lax.rem(a2 + o, 8)
             send(hub_full.at[t, core, a1, a2], hub_full.at[t, core, a1, a2], t, TWO_AG, base2 + g * stride2, j)
 
     def hub_back_one(t):
         wait_in(two_in.at[t], t, TWO_AG)
-        for o in (1, 7, 2, 6, 3, 5, 4):
+        for o in AROUND:
             g = lax.rem(a1 + o, 8)
             send(hub_full.at[t, core, a1], hub_full.at[t, core, a1], t, ONE_AG, base1 + g * stride1, j)
 
@@ -191,17 +246,19 @@
         low = lanes(x.shape) < 64
         return jnp.concatenate([jnp.where(low, x, 0.0), jnp.where(low, 0.0, x)], axis=0)
 
-    def tail_start(t, half):
-        bh, bl = split(halves(mine(half)))
+    def tail_start(t, doubled, between):
+        bh, bl = split(halves(doubled))
         both = side_by_side(bh, bl)
         for q in range(4):
             part = slice(256 * q, 256 * q + 256)
             x = fold(dot(tile_hi[part], both)) + dot(tile_lo[part], bh)
             tail_send[t, 32 * q:32 * q + 32] = x.reshape(32, 8, 128)
         tail_recv[t, d] = tail_send[t, d]
-        peers_all(lambda p: send(tail_send.at[t, p], tail_recv.at[t, d], t, TAIL_F, p, j))
-
-    def tail_turn(t):
+        around(lambda p: send(tail_send.at[t, p], tail_recv.at[t, d], t, TAIL_F, p, j), (0,))
+        between()
+        around(lambda p: send(tail_send.at[t, p], tail_recv.at[t, d], t, TAIL_F, p, j), (1,))
+
+    def tail_turn(t, between):
         wait_in(tail_recv.at[t, pl.ds(0, 127)], t, TAIL_F)
         hi, lo = split(tail_recv[t].reshape(1024, 128))
         x = fold(dot(member[...], side_by_side(hi, lo)))
@@ -215,7 +272,9 @@
             x = fold(dot(member_t[256 * q:256 * q + 256], both))
             reply_send[t, 32 * q:32 * q + 32] = x.reshape(32, 8, 128)
         reply_recv[t, d] = reply_send[t, d]
-        peers_all(lambda p: send(reply_send.at[t, p], reply_recv.at[t, d], t, TAIL_R, p, j))
+        around(lambda p: send(reply_send.at[t, p], reply_recv.at[t, d], t, TAIL_R, p, j), (0,))
+        between()
+        around(lambda p: send(reply_send.at[t, p], reply_recv.at[t, d], t, TAIL_R, p, j), (1,))
         if t == 1:
             tail_pack[j] = jnp.where(lanes((128, 128)) < 64, item[:128], item[128:])
             peers_hub(lambda h, o: send(tail_pack.at[j], tail_pack.at[j], 0, TAIL_OUT, d, h))
@@ -229,8 +288,14 @@
 
     def join(t, packed):
         wait_in(user_in.at[t], t, HUB_RS)
-        grad_pack[t, j] = packed + user_pack[t, j] + user_in[t, 0] + user_in[t, 1] + user_in[t, 2]
+        packed = packed + user_pack[t, j] + user_in[t, 0] + user_in[t, 1] + user_in[t, 2]
+        grad_pack[t, j] = packed
         peers_hub(lambda h, o: send(grad_pack.at[t, j], grad_pack.at[t, j], t, HUB_AG, d, h))
+        low = lanes((64, 128)) < 64
+        turned = roll64(packed)
+        return jnp.concatenate([jnp.where(low, packed, turned), jnp.where(low, turned, packed)], axis=0)
+
+    def unpack(t):
         wait_in(user_in.at[t], t, HUB_AG)
         low = lanes((64, 128)) < 64
         out = user_out if t == 1 else grad_ref
@@ -240,12 +305,18 @@
             out[64:, 128 * k:128 * k + 128] = jnp.where(low, roll64(even), uneven)
 
     hub_start(0, cot_ref[...])
-    wait_in(tile_in, 0, TILE_RS)
-    own = pl.ds(j * 32, 32)
-    tile_sum[own] = tiles_ref[own] + tile_in[0] + tile_in[1] + tile_in[2]
-    peers_hub(lambda h, o: send(tile_sum.at[own], tile_sum.at[own], 0, TILE_AG, d, h))
+    for i in range(CUTS):
+        wait_in(tile_in.at[i], 0, TILE_RS + 2 * i)
+        own = pl.ds(j * 32 + i * cut, cut)
+        tile_sum[own] = tiles_ref[own] + tile_in[i, 0] + tile_in[i, 1] + tile_in[i, 2]
+        peers_hub(lambda h, o: send(tile_sum.at[own], tile_sum.at[own], 0, TILE_AG + 2 * i, d, h))
+    wait_in(index_mid.at[pl.ds(0, 15)], 0, INDEX_ONE)
+    along_two(lambda g, p: send(index_mid, index_in.at[a2], 0, INDEX_TWO, p, j))
+    index_in[a2] = index_mid[...]
     hub_one(0)
-    wait_in(tile_in, 0, TILE_AG)
+    hub_two(0)
+    for i in range(CUTS):
+        wait_in(tile_in.at[i], 0, TILE_AG + 2 * i)
 
     th, tl = split(tile_sum[...].reshape(128, 1024))
     both = jnp.concatenate([th, tl], axis=1)
@@ -258,13 +329,16 @@
         hi, lo = split(placed.T)
         tile_t_hi[128 * s:128 * s + 128] = hi
         tile_t_lo[128 * s:128 * s + 128] = lo
-    tail_start(0, cot_ref[:, pl.ds(left_half, 128)])
-    hub_two(0)
-
-    wait_in(index_in.at[pl.ds(0, 127)], 0, INDEX)
-    spread = (rows((1024, 128)) // 8 == lanes((1024, 128))).astype(BF16)
+    tail_start(0, mine(cot_ref[:, pl.ds(left_half, 128)]), lambda: hub_back_two(0))
+
+    wait_in(index_in.at[pl.ds(0, 7)], 0, INDEX_TWO)
+    shape = (1024, 128)
+    sender = rows(shape) // 8
+    turned = 16 * lax.rem(sender // 2, 8) + 2 * (sender // 16) + lax.rem(sender, 2)
+    spread = (sender * (1 - core) + turned * core == lanes(shape)).astype(BF16)
     blocks = dot(spread, index_in[...].reshape(128, 128).astype(BF16))
-    place = blocks * 8.0 + lax.rem(rows((1024, 128)), 8).astype(F32)
+    chosen = [jnp.sum(jnp.where(lanes(shape) == 2 * a2 + s, blocks, 0.0), axis=1, keepdims=True) for s in range(2)]
+    place = jnp.where(lanes(shape) < 64, chosen[0], chosen[1]) * 8.0 + lax.rem(rows(shape), 8).astype(F32)
     place_t = place.T
     want_t = lanes((1024, 256)).astype(F32)
     want = rows((256, 1024)).astype(F32)
@@ -272,18 +346,23 @@
         member_t[:, 256 * s:256 * s + 256] = (place[:, 64 * s:64 * s + 1] == want_t).astype(F32).astype(BF16)
         member[256 * s:256 * s + 256] = (place_t[64 * s:64 * s + 1] == want).astype(F32).astype(BF16)
 
-    for t in range(2):
-        if t == 1:
-            hub_start(1, grad_ref[...])
-            tail_start(1, grad_ref[:, pl.ds(left_half, 128)])
-            hub_one(1)
-            hub_two(1)
-        hub_back_two(t)
-        hub_back_one(t)
-        hub_back_pair(t)
-        tail_turn(t)
-        hub_finish(t)
-        join(t, tail_end(t))
+    hub_back_one(0)
+    tail_turn(0, lambda: hub_back_pair(0))
+    hub_finish(0)
+
+    def hub_again():
+        unpack(0)
+        hub_start(1, grad_ref[...])
+        hub_one(1)
+
+    tail_start(1, join(0, tail_end(0)), hub_again)
+    hub_two(1)
+    tail_turn(1, lambda: hub_back_two(1))
+    hub_back_one(1)
+    hub_back_pair(1)
+    hub_finish(1)
+    join(1, tail_end(1))
+    unpack(1)
 
     wait_in(tail_pack.at[pl.ds(0, 3)], 0, TAIL_OUT)
     low = lanes((128, 128)) < 64
@@ -292,9 +371,10 @@
         tail_out[:128, 128 * k:128 * k + 128] = jnp.where(low, even, roll64(uneven))
         tail_out[128:, 128 * k:128 * k + 128] = jnp.where(low, roll64(even), uneven)
 
-    wait_out(tile_in, 0, TILE_RS)
-    wait_out(tile_in, 0, TILE_AG)
-    wait_out(index_in.at[pl.ds(0, 127)], 0, INDEX)
+    for i in range(2 * CUTS):
+        wait_out(tile_in.at[0], 0, TILE_RS + i)
+    wait_out(index_mid.at[pl.ds(0, 15)], 0, INDEX_ONE)
+    wait_out(index_in.at[pl.ds(0, 7)], 0, INDEX_TWO)
     wait_out(tail_pack.at[pl.ds(0, 3)], 0, TAIL_OUT)
     for t in range(2):
         wait_out(pair_in.at[t], t, PAIR_RS)
@@ -318,13 +398,21 @@
             jax.ShapeDtypeStruct((512, 256), F32),
             jax.ShapeDtypeStruct((256, 256), F32),
         ),
-        in_specs=[vmem] * 6,
+        in_specs=[pl.BlockSpec(memory_space=pltpu.HBM)] * 6,
         out_specs=(vmem,) * 3,
         scratch_shapes=[
-            pltpu.VMEM((3, 32, 8, 128), F32),
+            pltpu.VMEM((128, 256), F32),
+            pltpu.VMEM((128, 512), F32),
             pltpu.VMEM((128, 8, 128), F32),
-            pltpu.VMEM((128, 1, 128), F32),
-            pltpu.VMEM((128, 1, 128), F32),
+            pltpu.VMEM((3, 128), jnp.int32),
+            pltpu.VMEM((2, 512, 256), jnp.int32),
+            pltpu.VMEM((2, 256, 256), jnp.int32),
+            pltpu.SemaphoreType.DMA((6,)),
+            pltpu.VMEM((CUTS, 3, 32 // CUTS, 8, 128), F32),
+            pltpu.VMEM((128, 8, 128), F32),
+            pltpu.VMEM((2, 8, 1, 128), F32),
+            pltpu.VMEM((16, 1, 128), F32),
+            pltpu.VMEM((8, 16, 1, 128), F32),
             pltpu.VMEM((1024, 256), BF16),
             pltpu.VMEM((1024, 256), BF16),
             pltpu.VMEM((256, 1024), BF16),

time: 147 us -> 125 us (0.85)
  Pallas kernels: 138 us -> 116 us
    pallas_call x1, Pallas kernels: 138 us -> 116 us  [local(): pl.pallas_call(kernel, out_shape=(jax.ShapeDtypeStruct((128, 256), F32),...]
where the time goes in v2:
time: 125 us
  Pallas kernels  116 us (93%)
  local copies, waits for them, and re-layouts  7.99 us (6%)
    pallas_call x1, Pallas kernels, local(): pl.pallas_call(kernel, out_shape=(jax.ShapeDtypeStruct((128, 256), F32),...  116 us
    unnamed x15, local copies, waits for them, and re-layouts  7.99 us

profile of v2, /device:TPU:1, one launch (start us, length us, event | category | flops | bytes accessed | tf_op | source)
XLA Modules:
  0.0 124.8 jit_solution(9595029060983669569)
XLA Ops:
  0.6 0.0 copy-start
  0.6 1.2 copy-done
  1.9 0.0 copy-start.1
  1.9 1.0 copy-done.1
  2.9 0.0 copy-start.2
  2.9 1.0 copy-done.2
  3.9 0.0 copy-start.3
  3.9 0.9 copy-done.3
  4.9 0.0 copy-start.4
  4.9 0.9 copy-done.4
  5.8 0.0 copy-start.5
  5.8 0.7 copy-done.5
  6.5 116.1 %shard_map.85 = (f32[128,256]{1,0:T(8,128)S(1)}, f32[512,256]{1,0:T(8,128)S(1)}, f32[256,256]{1,0:T(8,128)S(1)}) custom-call(f32[128,256]{1,0:T(8,128)S(1)} %copy-done.4, f32[128,512]{1,0:T(8,128)S(1)} %copy-done.3, f32[128,8,128]{2,1,0:T(8,128)S(1)} %copy-done.1, s32[3,128]{1,0:T(4,128)S(1)} %copy-done.5, s32[2,512,256]{2,1,0:T(8,128)S(1)} %copy-done, ...), custom_call_target="tpu_custom_call" | custom-call | flops 4000000000 | bytes 4000000 | tf_op jit(solution)/shard_map/pallas_call | solution.py:394
  122.6 0.7 copy.12
  123.3 0.8 copy.13
  124.1 0.7 copy.14
Async XLA Ops:
  0.6 1.2 copy-start
  1.9 1.0 copy-start.1
  2.9 1.0 copy-start.2
  3.9 0.9 copy-start.3
  4.9 0.9 copy-start.4
  5.8 0.7 copy-start.5

commit v3 on v2

--- a/solution.py
+++ b/solution.py
@@ -56,7 +56,7 @@
     tile_in, tile_sum, slot_index, index_mid, index_in, tile_hi, tile_lo, tile_t_hi, tile_t_lo, member, member_t,
     hubp, pair_in, one_out, one_in, two_out, two_in, hub_full,
     tail_send, tail_recv, reply_send, reply_recv, user_pack, user_in, grad_pack, tail_pack, grad_ref,
-    send_sem, recv_sem,
+    send_sem, recv_sem, ready_sem,
 ):
     d = lax.axis_index("dom")
     j = lax.axis_index("hub")
@@ -121,16 +121,26 @@
     for load in loads:
         load.start()
     barrier = pltpu.get_barrier_semaphore()
-    around(lambda p: pl.semaphore_signal(barrier, inc=1, device_id=(p, j), device_id_type=MESH))
+    for o in AROUND:
+        g, h = lax.rem(y + o, 8), lax.rem(z + o, 8)
+        for c in range(2):
+            for p in (16 * z + 2 * g + c, 16 * h + 2 * y + c):
+                pl.semaphore_signal(barrier, inc=1, device_id=(p, j), device_id_type=MESH)
+    pl.semaphore_signal(barrier, inc=1, device_id=(partner, j), device_id_type=MESH)
     peers_hub(lambda h, o: pl.semaphore_signal(barrier, inc=1, device_id=(d, h), device_id_type=MESH))
     for load in loads:
         load.wait()
-    pl.semaphore_wait(barrier, 130)
+    pl.semaphore_wait(barrier, 32)
 
     cut = 32 // CUTS
     for i in range(CUTS):
         peers_hub(lambda h, o: send(
             tiles_ref.at[pl.ds(h * 32 + i * cut, cut)], tile_in.at[i, o], 0, TILE_RS + 2 * i, d, h))
+
+    for o in AROUND:
+        pl.semaphore_signal(
+            ready_sem, inc=1, device_id=(16 * lax.rem(z + o, 8) + 2 * y + core, j), device_id_type=MESH
+        )
 
     owner_row = jnp.broadcast_to(index_ref[1:2, :], (128, 128))
     block_row = jnp.broadcast_to(index_ref[2:3, :], (128, 128)).astype(F32)
@@ -305,6 +315,7 @@
             out[64:, 128 * k:128 * k + 128] = jnp.where(low, roll64(even), uneven)
 
     hub_start(0, cot_ref[...])
+    hub_one(0)
     for i in range(CUTS):
         wait_in(tile_in.at[i], 0, TILE_RS + 2 * i)
         own = pl.ds(j * 32 + i * cut, cut)
@@ -313,7 +324,6 @@
     wait_in(index_mid.at[pl.ds(0, 15)], 0, INDEX_ONE)
     along_two(lambda g, p: send(index_mid, index_in.at[a2], 0, INDEX_TWO, p, j))
     index_in[a2] = index_mid[...]
-    hub_one(0)
     hub_two(0)
     for i in range(CUTS):
         wait_in(tile_in.at[i], 0, TILE_AG + 2 * i)
@@ -329,6 +339,7 @@
         hi, lo = split(placed.T)
         tile_t_hi[128 * s:128 * s + 128] = hi
         tile_t_lo[128 * s:128 * s + 128] = lo
+    pl.semaphore_wait(ready_sem, 7)
     tail_start(0, mine(cot_ref[:, pl.ds(left_half, 128)]), lambda: hub_back_two(0))
 
     wait_in(index_in.at[pl.ds(0, 7)], 0, INDEX_TWO)
@@ -437,6 +448,7 @@
             pltpu.VMEM((128, 256), F32),
             pltpu.SemaphoreType.DMA((2, KINDS)),
             pltpu.SemaphoreType.DMA((2, KINDS)),
+            pltpu.SemaphoreType.REGULAR,
         ],
         compiler_params=pltpu.CompilerParams(
             collective_id=0, has_side_effects=True, vmem_limit_bytes=48 * 1024 * 1024

time: 125 us -> 122 us (0.976)
  Pallas kernels: 116 us -> 113 us
    pallas_call x1, Pallas kernels: 116 us -> 113 us  [local(): pl.pallas_call(kernel, out_shape=(jax.ShapeDtypeStruct((128, 256), F32),...]
where the time goes in v3:
time: 122 us; the launch traced here: 121 us
  Pallas kernels  113 us (93%)
  local copies, waits for them, and re-layouts  7.99 us (7%)
    pallas_call x1, Pallas kernels, local(): pl.pallas_call(kernel, out_shape=(jax.ShapeDtypeStruct((128, 256), F32),...  113 us
    unnamed x15, local copies, waits for them, and re-layouts  7.99 us

profile of v3, /device:TPU:1, one launch (start us, length us, event | category | flops | bytes accessed | tf_op | source)
XLA Modules:
  0.0 121.2 jit_solution(16054804466673556554)
XLA Ops:
  0.6 0.0 copy-start
  0.6 1.2 %copy-done = s32[2,512,256]{2,1,0:T(8,128)S(1)} copy-done((s32[2,512,256]{2,1,0:T(8,128)S(1)}, s32[2,512,256]{2,1,0:T(8,128)}, u32[]{:S(2)}) %copy-start) | copy-done | bytes 1048600
  1.9 0.0 copy-start.1
  1.9 1.0 copy-done.1
  2.9 0.0 copy-start.2
  2.9 1.0 copy-done.2
  3.9 0.0 copy-start.3
  3.9 0.9 copy-done.3
  4.9 0.0 copy-start.4
  4.9 0.9 copy-done.4
  5.8 0.0 copy-start.5
  5.8 0.7 copy-done.5
  6.5 112.5 %shard_map.85 = (f32[128,256]{1,0:T(8,128)S(1)}, f32[512,256]{1,0:T(8,128)S(1)}, f32[256,256]{1,0:T(8,128)S(1)}) custom-call(f32[128,256]{1,0:T(8,128)S(1)} %copy-done.4, f32[128,512]{1,0:T(8,128)S(1)} %copy-done.3, f32[128,8,128]{2,1,0:T(8,128)S(1)} %copy-done.1, s32[3,128]{1,0:T(4,128)S(1)} %copy-done.5, s32[2,512,256]{2,1,0:T(8,128)S(1)} %copy-done, ...), custom_call_target="tpu_custom_call" | custom-call | flops 4000000000 | bytes 4000000 | tf_op jit(solution)/shard_map/pallas_call | solution.py:405
  119.0 0.7 copy.12
  119.7 0.8 copy.13
  120.5 0.7 copy.14
Async XLA Ops:
  0.6 1.2 %copy-start = (s32[2,512,256]{2,1,0:T(8,128)S(1)}, s32[2,512,256]{2,1,0:T(8,128)}, u32[]{:S(2)}) copy-start(s32[2,512,256]{2,1,0:T(8,128)} %hub_mask_hbm.1) | copy-start | bytes 3145732
  1.9 1.0 copy-start.1
  2.9 1.0 copy-start.2
  3.9 0.9 copy-start.3
  4.9 0.9 copy-start.4
  5.8 0.7 copy-start.5
